TPU v7x, 512 devices: a whole 4x4x16 slice. The times are simulated.
512 devices in a mesh: tile: 128 (over y_lo, x, z), dir: 4 (over y_hi, core).
Axes of the slice: x: 4, y: 4 (y_hi: 2, y_lo: 2; y = y_hi * 2 + y_lo), z: 16, core: 2. Of those that a mesh axis runs over, the one named last changes fastest.
Arguments:
- layers: bfloat16 [4, 16384, 2048], P('dir', 'tile'), may hold values from -6 to 6
- offsets: int32 [4, 4, 2], replicated, may hold values from 0 to 8191, as said below
- subap_valid: int32 [128, 16], P('tile'), may hold values from 0 to 1, as said below
- defocus: float32 [3], replicated, may hold values from -0.08 to 0.08
- weights: float32 [3], replicated, may hold values from 0.25 to 1
Outputs:
- spots: bfloat16 [4, 128, 128, 2048], P('dir', 'tile')
Inputs may be any that keep to these rules, and one draw needn't show every extreme that they name: offsets[d, l, 0] < 1024 and offsets[d, l, 1] < 8192; both bounds minus one are taken by some pair in every draw. `subap_valid`: the part of an annulus of lit subapertures that falls in the strip, with a few dead ones.
All inputs are finite; a program needn't handle non-finite values.
Results may differ from a plain program's by a relative error of at most 0.0055.
Values may be sent and summed in bfloat16 or wider, within the bound.
No kernel may reach another device: no remote copies, remote signals or barrier semaphores. Data moves between devices by JAX's collectives and lax.ppermute only.
A program may use at most 64 MiB of HBM per device.

v0:
```python
import math
import jax
import jax.numpy as jnp
from jax import lax
from jax.sharding import PartitionSpec as P

SUBPIX = 128
SPOT = 128
SUBX = 16
SLICES = 3
REACH = 2
QUANT = 4
OVER = 2
PCOLS = 2048


def shifted(value, axis, by):
    count = lax.axis_size(axis)
    return lax.ppermute(value, axis, [(i, (i + by) % count) for i in range(count)])


def tables():
    frequency = jnp.arange(SPOT, dtype=jnp.float32) - SPOT // 2
    position = jnp.arange(SUBPIX, dtype=jnp.float32) - (SUBPIX - 1) / 2.0
    phase_angle = -2.0 * math.pi / (OVER * SUBPIX) * frequency[:, None] * position[None, :]
    factor = 1.0 / math.sqrt(SUBPIX)
    real_part = jnp.cos(phase_angle) * factor
    imag_part = jnp.sin(phase_angle) * factor
    left_table = jnp.concatenate(
        [jnp.concatenate([real_part, -imag_part], 1), jnp.concatenate([imag_part, real_part], 1)], 0
    ).astype(jnp.bfloat16)
    right_table = jnp.concatenate(
        [
            jnp.concatenate([real_part.T, imag_part.T], 1),
            jnp.concatenate([-imag_part.T, real_part.T], 1),
        ],
        0,
    ).astype(jnp.bfloat16)
    return (left_table, right_table)


def interpolate(window, offset_pair):
    col_steps = offset_pair[1] // QUANT
    col_frac = (offset_pair[1] % QUANT).astype(jnp.float32) / QUANT
    row_frac = (offset_pair[0] % QUANT).astype(jnp.float32) / QUANT
    col_first = jnp.roll(window, -col_steps, axis=1)
    col_second = jnp.roll(window, -(col_steps + 1), axis=1)
    across = (1.0 - col_frac) * col_first + col_frac * col_second
    return ((1.0 - row_frac) * across[:-1] + row_frac * across[1:]).astype(jnp.bfloat16)


def spots_row(pupil_phase, first_row, total_rows, defocus, weights, valid_row):
    left_table, right_table = tables()
    row_position = (
        (first_row + jnp.arange(SUBPIX, dtype=jnp.int32)).astype(jnp.float32)
        - (total_rows - 1) / 2.0
    ) / SUBPIX
    col_position = (jnp.arange(PCOLS, dtype=jnp.float32) - (PCOLS - 1) / 2.0) / SUBPIX
    radius = row_position[:, None] ** 2 + col_position[None, :] ** 2
    spot_sum = jnp.zeros((SPOT * SUBX, SPOT), jnp.float32)
    for altitude in range(SLICES):
        phase_angle = pupil_phase + defocus[altitude] * radius
        pupil_field = jnp.concatenate([jnp.cos(phase_angle), jnp.sin(phase_angle)], 0).astype(
            jnp.bfloat16
        )
        focal_plane = jnp.dot(left_table, pupil_field, preferred_element_type=jnp.float32).astype(
            jnp.bfloat16
        )
        blocks = jnp.concatenate(
            [
                focal_plane[:SPOT].reshape(SPOT * SUBX, SUBPIX),
                focal_plane[SPOT:].reshape(SPOT * SUBX, SUBPIX),
            ],
            1,
        )
        spot_field = jnp.dot(blocks, right_table, preferred_element_type=jnp.float32)
        spot_sum = spot_sum + weights[altitude] * (
            spot_field[:, :SPOT] ** 2 + spot_field[:, SPOT:] ** 2
        )
    scaled = spot_sum / jnp.sum(weights)
    masked = scaled.reshape(SPOT, SUBX, SPOT) * valid_row.astype(jnp.float32)[None, :, None]
    return masked.reshape(SPOT, SUBX * SPOT).astype(jnp.bfloat16)


def extend(block):
    pieces = [block]
    for distance in range(1, REACH + 1):
        pieces.append(shifted(block, "tile", -distance))
    return jnp.concatenate(pieces, 1)


def shifted_term(extended, offset_pair):
    window = lax.dynamic_slice_in_dim(extended, offset_pair[0] // QUANT, SUBPIX + 1, 0).astype(
        jnp.float32
    )
    return interpolate(window, offset_pair)


def shards(layers, offsets, subap_valid, defocus, weights):
    own_dir = lax.axis_index("dir")
    tile_index = lax.axis_index("tile")
    total_rows = lax.axis_size("tile") * SUBPIX
    pupil_phase = jnp.zeros((SUBPIX, PCOLS), jnp.float32)
    stacked = lax.all_gather(layers, "dir", axis=0, tiled=True)
    extended = extend(stacked)
    offset_pairs = lax.dynamic_index_in_dim(offsets, own_dir, 0, keepdims=False)
    for layer_index in range(stacked.shape[0]):
        pupil_phase = pupil_phase + shifted_term(
            extended[layer_index], offset_pairs[layer_index]
        ).astype(jnp.float32)
    spots = spots_row(
        pupil_phase, tile_index * SUBPIX, total_rows, defocus, weights, subap_valid[0]
    )
    return spots[None, None]


def solution(mesh):
    placed = (P("dir", "tile", None), P(), P("tile", None), P(), P())
    return jax.shard_map(
        shards, mesh=mesh, in_specs=placed, out_specs=P("dir", "tile", None, None), check_vma=False
    )
```

profile of v0, /device:TPU:1, one launch (start us, length us, event | category | flops | bytes accessed | tf_op | source)
XLA Modules:
  0.0 236.5 jit_solution(6538307953497980572)
XLA Ops:
  6.5 0.7 all-gather.2.cloned.1.call-update
  7.3 42.3 %all-gather.2.cloned.1.call-done = bf16[4,128,2048]{2,1,0:T(8,128)(2,1)} async-done(((bf16[1,128,2048]{2,1,0:T(8,128)(2,1)}), bf16[4,128,2048]{2,1,0:T(8,128)(2,1)}) %all-gather.2.cloned.1.call-update) | async-done | bytes 2097168 | tf_op jit(solution)/shard_map/all_gather | solution.py:104
  49.5 7.8 %collective-permute-start = (bf16[4,128,2048]{2,1,0:T(8,128)(2,1)}, bf16[4,128,2048]{2,1,0:T(8,128)(2,1)}, u32[]{:S(2)}, u32[]{:S(2)}) collective-permute-start(bf16[4,128,2048]{2,1,0:T(8,128)(2,1)} %all-gather.2.cloned.1.call-done), channel_id=1, source_target_pairs={{0,508},{4,0},{8,4},{12,8},{16,12},{20,16},{24,20},{28,24},{32,28}... | collective-permute-start | bytes 6291464 | tf_op jit(solution)/shard_map/ppermute | solution.py:19
  57.4 3.8 %collective-permute-start.1 = (bf16[4,128,2048]{2,1,0:T(8,128)(2,1)}, bf16[4,128,2048]{2,1,0:T(8,128)(2,1)S(1)}, u32[]{:S(2)}, u32[]{:S(2)}) collective-permute-start(bf16[4,128,2048]{2,1,0:T(8,128)(2,1)} %all-gather.2.cloned.1.call-done), channel_id=1, source_target_pairs={{0,504},{4,508},{8,0},{12,4},{16,8},{20,12},{24,16},{28,20},{32,24... | collective-permute-start | bytes 6291464 | tf_op jit(solution)/shard_map/ppermute | solution.py:19
  61.2 0.7 fusion.83
  83.2 1.3 reduce_sum.9
  84.5 1.4 fusion.84
  85.9 1.4 fusion.85
  88.6 1.7 constant_dynamic-update-slice_fusion.2
  90.4 18.5 %collective-permute-done = bf16[4,128,2048]{2,1,0:T(8,128)(2,1)} collective-permute-done((bf16[4,128,2048]{2,1,0:T(8,128)(2,1)}, bf16[4,128,2048]{2,1,0:T(8,128)(2,1)}, u32[]{:S(2)}, u32[]{:S(2)}) %collective-permute-start) | collective-permute-done | bytes 2097184 | tf_op jit(solution)/shard_map/ppermute | solution.py:19
  108.9 1.7 constant_dynamic-update-slice_fusion.1
  110.6 81.7 %collective-permute-done.1 = bf16[4,128,2048]{2,1,0:T(8,128)(2,1)S(1)} collective-permute-done((bf16[4,128,2048]{2,1,0:T(8,128)(2,1)}, bf16[4,128,2048]{2,1,0:T(8,128)(2,1)S(1)}, u32[]{:S(2)}, u32[]{:S(2)}) %collective-permute-start.1) | collective-permute-done | bytes 2097184 | tf_op jit(solution)/shard_map/ppermute | solution.py:19
  192.4 1.0 fusion.79
  193.7 1.2 fusion.17
  195.0 1.2 fusion.12
  196.6 1.2 fusion.7
  197.8 1.2 fusion.2
  199.0 5.3 %cosine_convert_fusion.2 = (bf16[128,2048]{1,0:T(8,128)(2,1)S(1)}, f32[128,2048]{1,0:T(8,128)S(1)}) fusion(f32[2048]{0:T(1024)S(1)} %multiply_multiply_fusion, f32[128]{0:T(128)S(1)} %multiply_multiply_fusion.1, f32[]{:T(128)} %bitcast.17, f32[129,2048]{1,0:T(8,128)S(1)} %fusion.2, f32[]{:T(128)S(6)} %div.123, f32[]{:T(128)S(6)} %sub.110, ...), kind=kLoop, calls=%fused_computation.103 | loop fusion | flops 7077888 | bytes 9970212 | tf_op jit(solution)/shard_map/convert.14
  204.4 13.9 %sine_convert_fusion.2 = (bf16[128,2048]{1,0:T(8,128)(2,1)S(1)}, bf16[128,2048]{1,0:T(8,128)(2,1)S(1)}, bf16[128,2048]{1,0:T(8,128)(2,1)S(1)}, bf16[128,2048]{1,0:T(8,128)(2,1)}, bf16[128,2048]{1,0:T(8,128)(2,1)S(1)}) fusion(f32[128,2048]{1,0:T(8,128)S(1)} %get-tuple-element.7, f32[2048]{0:T(1024)S(1)} %multiply_multiply_fusion, ...), kind=kLoop, calls=%fused_computation.102 | loop fusion | flops 3145728 | bytes 3678732 | tf_op jit(solution)/shard_map/convert.15
  220.3 1.5 convolution_convert_fusion
  221.8 0.9 fusion.82
  223.0 1.3 reshape.134
  225.5 3.1 %fusion.26 = f32[2048,128]{1,0:T(8,128)S(1)} fusion(f32[2048,256]{1,0:T(8,128)S(1)} %fusion.57, f32[2048,256]{1,0:T(8,128)S(1)} %fusion.50, f32[2048,256]{1,0:T(8,128)S(1)} %fusion.43, f32[]{:T(128)} %reduce_sum.9, f32[]{:T(128)} %bitcast.20, f32[]{:T(128)} %bitcast.18, f32[]{:T(128)} %bitcast), kind=kLoop, calls=%fused_computation.49 | loop fusion | flops 3932160 | bytes 7340048 | tf_op jit(solution)/shard_map/div | solution.py:80
  228.8 0.9 multiply_convert_fusion
  (26 shorter events, 5.8 us)
Async XLA Ops:
  6.5 54.6 %copy-start = (s32[4,4,2]{1,2,0:T(2,128)S(1)}, s32[4,4,2]{1,2,0:T(2,128)}, u32[]{:S(2)}) copy-start(s32[4,4,2]{1,2,0:T(2,128)} %param.8) | copy-start | bytes 388
  6.5 43.0 %all-gather.2.cloned.1.call-start = ((), (), s32[]{:S(2)}) async-start(), calls=%async_computation | async-start | bytes 2621440 | tf_op jit(solution)/shard_map/all_gather | solution.py:104
  49.5 59.4 %collective-permute-start = (bf16[4,128,2048]{2,1,0:T(8,128)(2,1)}, bf16[4,128,2048]{2,1,0:T(8,128)(2,1)}, u32[]{:S(2)}, u32[]{:S(2)}) collective-permute-start(bf16[4,128,2048]{2,1,0:T(8,128)(2,1)} %all-gather.2.cloned.1.call-done), channel_id=1, source_target_pairs={{0,508},{4,0},{8,4},{12,8},{16,12},{20,16},{24,20},{28,24},{32,28}... | collective-permute-start | bytes 6291464 | tf_op jit(solution)/shard_map/ppermute | solution.py:19
  57.4 134.9 %collective-permute-start.1 = (bf16[4,128,2048]{2,1,0:T(8,128)(2,1)}, bf16[4,128,2048]{2,1,0:T(8,128)(2,1)S(1)}, u32[]{:S(2)}, u32[]{:S(2)}) collective-permute-start(bf16[4,128,2048]{2,1,0:T(8,128)(2,1)} %all-gather.2.cloned.1.call-done), channel_id=1, source_target_pairs={{0,504},{4,508},{8,0},{12,4},{16,8},{20,12},{24,16},{28,20},{32,24... | collective-permute-start | bytes 6291464 | tf_op jit(solution)/shard_map/ppermute | solution.py:19
Sparse Core Ops, SparseCore 0:
  9.5 40.0 all-gather.1
where the time goes:
time: 237 us
  waiting for transfers between devices  143 us (60%)
  between operations  34.9 us (15%)
  other arithmetic  31.4 us (13%)
  local copies, waits for them, and re-layouts  11.9 us (5%)
  starting transfers between devices  11.6 us (5%)
  matrix products  3.66 us (2%)
    ppermute x2, waiting for transfers between devices, shifted(): lax.ppermute(value, axis, [(i, (i + by) % count) for i in range(count)])  100 us
    all_gather x1, waiting for transfers between devices, shards(): stacked = lax.all_gather(layers, 'dir', axis=0, tiled=True)  42.3 us
    another operation x3, other arithmetic  19.8 us
    ppermute x2, starting transfers between devices, shifted(): lax.ppermute(value, axis, [(i, (i + by) % count) for i in range(count)])  11.6 us
    add x4, other arithmetic, interpolate(): across = (1.0 - col_frac) * col_first + col_frac * col_second  4.96 us
  transfers between devices with their start and end apart: 3, of which 3 were waited for; matrix products, arithmetic and copies ran while one was open for 4% of the time, Pallas kernels for 0%

commit v1 on v0

--- a/solution.py
+++ b/solution.py
@@ -101,7 +101,9 @@
     tile_index = lax.axis_index("tile")
     total_rows = lax.axis_size("tile") * SUBPIX
     pupil_phase = jnp.zeros((SUBPIX, PCOLS), jnp.float32)
-    stacked = lax.all_gather(layers, "dir", axis=0, tiled=True)
+    stacked = jnp.concatenate(
+        lax.all_to_all(jnp.stack([layers] * lax.axis_size("dir")), "dir", 0, 0), axis=0
+    )
     extended = extend(stacked)
     offset_pairs = lax.dynamic_index_in_dim(offsets, own_dir, 0, keepdims=False)
     for layer_index in range(stacked.shape[0]):

time: 237 us -> 222 us (0.937)
  waiting for transfers between devices: 143 us -> 106 us
  blocking collectives: 0 us -> 35.6 us
  between operations: 34.9 us -> 21.5 us
  local copies, waits for them, and re-layouts: 11.9 us -> 8.04 us
    all_gather x1 -> x0, waiting for transfers between devices: 42.3 us -> none  [shards(): stacked = lax.all_gather(layers, 'dir', axis=0, tiled=True)]
    all_to_all x0 -> x1, blocking collectives: none -> 35.6 us  [shards(): lax.all_to_all(jnp.stack([layers] * lax.axis_size('dir')), 'dir', 0, 0)]
    ppermute x2, waiting for transfers between devices: 100 us -> 106 us  [shifted(): lax.ppermute(value, axis, [(i, (i + by) % count) for i in range(count)])]
    unnamed x4 -> x8, local copies, waits for them, and re-layouts: 3.46 us -> 0.02 us
    concatenate x0 -> x1, other arithmetic: none -> 3.18 us  [extend(): return jnp.concatenate(pieces, 1)]
  transfers between devices with their start and end apart: 3 -> 2, of which waited for: 3 -> 2; matrix products, arithmetic and copies ran while one was open for 4% -> 1% of each run, Pallas kernels for 0% -> 0%
where the time goes in v1:
time: 222 us; the launch traced here: 221 us
  waiting for transfers between devices  106 us (48%)
  blocking collectives  35.6 us (16%)
  other arithmetic  33 us (15%)
  between operations  21.5 us (10%)
  starting transfers between devices  12.9 us (6%)
  local copies, waits for them, and re-layouts  8.04 us (4%)
  matrix products  3.68 us (2%)
    ppermute x2, waiting for transfers between devices, shifted(): lax.ppermute(value, axis, [(i, (i + by) % count) for i in range(count)])  106 us
    all_to_all x1, blocking collectives, shards(): lax.all_to_all(jnp.stack([layers] * lax.axis_size('dir')), 'dir', 0, 0)  35.6 us
    another operation x3, other arithmetic  19.6 us
    ppermute x2, starting transfers between devices, shifted(): lax.ppermute(value, axis, [(i, (i + by) % count) for i in range(count)])  12.9 us
    add x4, other arithmetic, interpolate(): across = (1.0 - col_frac) * col_first + col_frac * col_second  4.96 us
  transfers between devices with their start and end apart: 2, of which 2 were waited for; matrix products, arithmetic and copies ran while one was open for 1% of the time, Pallas kernels for 0%

profile of v1, /device:TPU:1, one launch (start us, length us, event | category | flops | bytes accessed | tf_op | source)
XLA Modules:
  0.0 220.9 jit_solution(1930579109794202567)
XLA Ops:
  0.0 1.3 stack.2
  1.3 35.6 %all_to_all.5 = bf16[4,1,128,2048]{3,2,1,0:T(8,128)(2,1)S(1)} all-to-all(bf16[4,1,128,2048]{3,2,1,0:T(8,128)(2,1)S(1)} %stack.2), channel_id=1, replica_groups=mesh['tile'=128,'dir'=4] {'dir'}, dimensions={0} | all-to-all | bytes 4194304 | tf_op jit(solution)/shard_map/all_to_all | solution.py:105
  37.0 9.8 %collective-permute-start = (bf16[4,128,2048]{2,1,0:T(8,128)(2,1)S(1)}, bf16[4,128,2048]{2,1,0:T(8,128)(2,1)}, u32[]{:S(2)}, u32[]{:S(2)}) collective-permute-start(bf16[4,128,2048]{2,1,0:T(8,128)(2,1)S(1)} %bitcast.32), channel_id=1, source_target_pairs={{0,508},{4,0},{8,4},{12,8},{16,12},{20,16},{24,20},{28,24},{32,28}... | collective-permute-start | bytes 6291464 | tf_op jit(solution)/shard_map/ppermute | solution.py:19
  46.8 3.1 %collective-permute-start.1 = (bf16[4,128,2048]{2,1,0:T(8,128)(2,1)S(1)}, bf16[4,128,2048]{2,1,0:T(8,128)(2,1)}, u32[]{:S(2)}, u32[]{:S(2)}) collective-permute-start(bf16[4,128,2048]{2,1,0:T(8,128)(2,1)S(1)} %bitcast.33), channel_id=1, source_target_pairs={{0,504},{4,508},{8,0},{12,4},{16,8},{20,12},{24,16},{28,20},{32,24... | collective-permute-start | bytes 6291464 | tf_op jit(solution)/shard_map/ppermute | solution.py:19
  50.0 0.7 fusion.83
  71.9 0.7 reduce_sum.9
  72.6 0.6 fusion.84
  73.2 0.7 fusion.85
  74.0 0.6 fusion.71
  74.6 20.2 %collective-permute-done = bf16[4,128,2048]{2,1,0:T(8,128)(2,1)} collective-permute-done((bf16[4,128,2048]{2,1,0:T(8,128)(2,1)S(1)}, bf16[4,128,2048]{2,1,0:T(8,128)(2,1)}, u32[]{:S(2)}, u32[]{:S(2)}) %collective-permute-start) | collective-permute-done | bytes 2097184 | tf_op jit(solution)/shard_map/ppermute | solution.py:19
  94.8 85.8 %collective-permute-done.1 = bf16[4,128,2048]{2,1,0:T(8,128)(2,1)} collective-permute-done((bf16[4,128,2048]{2,1,0:T(8,128)(2,1)S(1)}, bf16[4,128,2048]{2,1,0:T(8,128)(2,1)}, u32[]{:S(2)}, u32[]{:S(2)}) %collective-permute-start.1) | collective-permute-done | bytes 2097184 | tf_op jit(solution)/shard_map/ppermute | solution.py:19
  180.6 3.2 %pad_maximum_fusion = bf16[4,384,2048]{2,1,0:T(8,128)(2,1)S(1)} fusion(bf16[4,128,2048]{2,1,0:T(8,128)(2,1)} %collective-permute-done.1, bf16[4,128,2048]{2,1,0:T(8,128)(2,1)} %collective-permute-done, bf16[4,128,2048]{2,1,0:T(8,128)(2,1)S(1)} %bitcast.34), kind=kLoop, calls=%fused_computation | loop fusion | flops 18874368 | bytes 12582912 | tf_op jit(solution)/shard_map/concatenate | solution.py:89
  183.8 1.0 fusion.79
  185.1 1.2 fusion.17
  186.3 1.2 fusion.12
  187.9 1.2 fusion.7
  189.1 1.2 fusion.2
  190.4 5.1 %cosine_convert_fusion.2 = (bf16[128,2048]{1,0:T(8,128)(2,1)S(1)}, f32[128,2048]{1,0:T(8,128)S(1)}) fusion(f32[2048]{0:T(1024)S(1)} %multiply_multiply_fusion, f32[128]{0:T(128)S(1)} %multiply_multiply_fusion.1, f32[]{:T(128)} %bitcast.19, f32[129,2048]{1,0:T(8,128)S(1)} %fusion.2, f32[]{:T(128)S(6)} %div.123, f32[]{:T(128)S(6)} %sub.110, ...), kind=kLoop, calls=%fused_computation.104 | loop fusion | flops 7077888 | bytes 9970212 | tf_op jit(solution)/shard_map/convert.14
  195.5 13.9 %sine_convert_fusion.2 = (bf16[128,2048]{1,0:T(8,128)(2,1)S(1)}, bf16[128,2048]{1,0:T(8,128)(2,1)S(1)}, bf16[128,2048]{1,0:T(8,128)(2,1)S(1)}, bf16[128,2048]{1,0:T(8,128)(2,1)}, bf16[128,2048]{1,0:T(8,128)(2,1)S(1)}) fusion(f32[128,2048]{1,0:T(8,128)S(1)} %get-tuple-element.7, f32[2048]{0:T(1024)S(1)} %multiply_multiply_fusion, ...), kind=kLoop, calls=%fused_computation.103 | loop fusion | flops 3145728 | bytes 3678732 | tf_op jit(solution)/shard_map/convert.15
  211.5 1.5 convolution_convert_fusion
  213.0 0.9 fusion.82
  214.1 1.3 reshape.141
  216.7 3.1 %fusion.26 = f32[2048,128]{1,0:T(8,128)S(1)} fusion(f32[2048,256]{1,0:T(8,128)S(1)} %fusion.57, f32[2048,256]{1,0:T(8,128)S(1)} %fusion.50, f32[2048,256]{1,0:T(8,128)S(1)} %fusion.43, f32[]{:T(128)} %reduce_sum.9, f32[]{:T(128)} %bitcast.22, f32[]{:T(128)} %bitcast.20, f32[]{:T(128)} %bitcast), kind=kLoop, calls=%fused_computation.50 | loop fusion | flops 3932160 | bytes 7340048 | tf_op jit(solution)/shard_map/div | solution.py:80
  220.0 0.9 multiply_convert_fusion
  (29 shorter events, 4.5 us)
Async XLA Ops:
  0.0 49.9 %copy-start = (s32[4,4,2]{1,2,0:T(2,128)S(1)}, s32[4,4,2]{1,2,0:T(2,128)}, u32[]{:S(2)}) copy-start(s32[4,4,2]{1,2,0:T(2,128)} %param.8) | copy-start | bytes 388
  1.3 70.6 %copy-start.1 = (f32[3]{0:T(128)S(1)}, f32[3]{0:T(128)}, u32[]{:S(2)}) copy-start(f32[3]{0:T(128)} %param.11) | copy-start | bytes 40
  1.3 71.9 %copy-start.2 = (f32[3]{0:T(128)S(1)}, f32[3]{0:T(128)}, u32[]{:S(2)}) copy-start(f32[3]{0:T(128)} %param.10) | copy-start | bytes 40
  1.3 72.6 %copy-start.3 = (s32[1,16]{1,0:T(1,128)S(1)}, s32[1,16]{1,0:T(1,128)}, u32[]{:S(2)}) copy-start(s32[1,16]{1,0:T(1,128)} %param.9) | copy-start | bytes 196
  37.0 57.8 %collective-permute-start = (bf16[4,128,2048]{2,1,0:T(8,128)(2,1)S(1)}, bf16[4,128,2048]{2,1,0:T(8,128)(2,1)}, u32[]{:S(2)}, u32[]{:S(2)}) collective-permute-start(bf16[4,128,2048]{2,1,0:T(8,128)(2,1)S(1)} %bitcast.32), channel_id=1, source_target_pairs={{0,508},{4,0},{8,4},{12,8},{16,12},{20,16},{24,20},{28,24},{32,28}... | collective-permute-start | bytes 6291464 | tf_op jit(solution)/shard_map/ppermute | solution.py:19
  46.8 133.7 %collective-permute-start.1 = (bf16[4,128,2048]{2,1,0:T(8,128)(2,1)S(1)}, bf16[4,128,2048]{2,1,0:T(8,128)(2,1)}, u32[]{:S(2)}, u32[]{:S(2)}) collective-permute-start(bf16[4,128,2048]{2,1,0:T(8,128)(2,1)S(1)} %bitcast.33), channel_id=1, source_target_pairs={{0,504},{4,508},{8,0},{12,4},{16,8},{20,12},{24,16},{28,20},{32,24... | collective-permute-start | bytes 6291464 | tf_op jit(solution)/shard_map/ppermute | solution.py:19
